TPU v7x, 32 devices: a whole 2x2x4 slice. The times are simulated.
32 devices in a mesh: grp: 4 (over x, core), sub: 8 (over z, y).
Axes of the slice: x: 2, y: 2, z: 4, core: 2. Of those that a mesh axis runs over, the one named last changes fastest.
Arguments:
- right_side: float32 [65536, 128], P(('grp', 'sub')), may hold values from -6 to 6
- fine_values: float32 [81, 65536], P(None, ('grp', 'sub')), as said below
- columns: int32 [81, 65536], P(None, ('grp', 'sub')), may hold values from 0 to 2175, as said below
- agg_map: int32 [65536], P(('grp', 'sub')), may hold values from 0 to 127
- send_lo: int32 [2048], P(('grp', 'sub')), may hold values from 0 to 2047
- send_hi: int32 [2048], P(('grp', 'sub')), may hold values from 0 to 2047
- coarse_matrix: float32 [4, 1024, 1024], P('grp', 'sub'), as said below
Outputs:
- solution: float32 [65536, 128], P(('grp', 'sub'))
- residual: float32 [65536, 128], P(('grp', 'sub'))
Inputs may be any that keep to these rules, and one draw needn't show every extreme that they name: `columns`: entry 0 of row i of a partition is 64 + i, the others lie within 64 positions of it. `fine_values`: entry 0 lies in 2.5 to 5 and every other entry's magnitude is at most 0.06. `coarse_matrix`: symmetric; the diagonal lies in 10 to 20, other entries' magnitudes are at most 7.1 / sqrt(1024).
All inputs are finite; a program needn't handle non-finite values.
Results may differ from a plain program's by a relative error of at most 0.0001.
Values sent between devices are 32-bit elements; how exact they have to be, the bound alone decides.
A program may use at most 128 MiB of HBM per device.

v0:
```python
import jax
import jax.numpy as jnp
from jax import lax
from jax.sharding import PartitionSpec as P

CHEB_FINE = 2
CHEB_COARSE = 6
CYCLES = 2
THETA = 1.0
DELTA = 0.7
OMEGA = 0.6
highest = lax.Precision.HIGHEST


def from_behind(shard, axis, by):
    peers = lax.axis_size(axis)
    pairs = [(i, i + by) for i in range(peers) if 0 <= i + by < peers]
    return lax.ppermute(shard, axis, pairs)


def band_tiles(fine_values, columns, block_rows):
    rows_dev = columns.shape[1]
    rows = jnp.arange(rows_dev, dtype=jnp.int32)
    starts = rows // block_rows * block_rows
    local = columns - starts[None, :]
    places = jnp.arange(2 * block_rows, dtype=jnp.int32)[None, :]
    tiles = jnp.zeros((rows_dev, 2 * block_rows), jnp.float32)
    for entry in range(columns.shape[0]):
        tiles = tiles + jnp.where(local[entry][:, None] == places, fine_values[entry][:, None], 0.0)
    tiles = tiles.reshape(rows_dev // block_rows, block_rows, 2 * block_rows)
    return (tiles[:, :, :block_rows], tiles[:, :, block_rows:])


def selector(indices, count):
    return (indices[:, None] == jnp.arange(count, dtype=jnp.int32)[None, :]).astype(jnp.float32)


def fine_apply(vector, low_tiles, high_tiles, pick_lo, pick_hi):
    upper_rows = jnp.dot(pick_hi, vector, precision=highest)
    lower_rows = jnp.dot(pick_lo, vector, precision=highest)
    below = from_behind(upper_rows, ("grp", "sub"), 1)
    above = from_behind(lower_rows, ("grp", "sub"), -1)
    extended = jnp.concatenate([below, vector, above], 0)
    block_rows = low_tiles.shape[1]
    pieces = extended.reshape(-1, block_rows, vector.shape[1])
    total = jnp.einsum("brc,bcn->brn", low_tiles, pieces[:-1], precision=highest)
    total = total + jnp.einsum("brc,bcn->brn", high_tiles, pieces[1:], precision=highest)
    return total.reshape(vector.shape)


def chebyshev(residual, apply, inverse, steps, final):
    rho_old = DELTA / THETA
    direction = inverse * residual / THETA
    result = direction
    for turn in range(1, steps):
        residual = residual - apply(direction)
        rho_new = 1.0 / (2.0 * THETA / DELTA - rho_old)
        direction = rho_new * rho_old * direction + 2.0 * rho_new / DELTA * inverse * residual
        result = result + direction
        rho_old = rho_new
    if final:
        residual = residual - apply(direction)
    return (result, residual)


def body(right_side, fine_values, columns, agg_map, send_lo, send_hi, coarse_matrix):
    rows_dev = right_side.shape[0]
    low_tiles, high_tiles = band_tiles(fine_values, columns, 2 * send_lo.shape[0])
    pick_lo = selector(send_lo, rows_dev)
    pick_hi = selector(send_hi, rows_dev)

    def apply_fine(vector):
        return fine_apply(vector, low_tiles, high_tiles, pick_lo, pick_hi)

    own_rows = coarse_matrix[0]
    aggregates = own_rows.shape[0]
    sub_index = lax.axis_index("sub")
    start = sub_index * aggregates
    block = lax.dynamic_slice_in_dim(own_rows, start, aggregates, 1)
    coarse_inverse = 1.0 / jnp.diagonal(block)[:, None]

    def apply_coarse(vector):
        whole = lax.all_gather(vector, "sub", axis=0, tiled=True)
        return jnp.dot(own_rows, whole, precision=highest)

    dinv = 1.0 / fine_values[0][:, None]
    onehot = selector(agg_map, aggregates)
    solution = jnp.zeros_like(right_side)
    residual = right_side
    for cycle in range(CYCLES):
        update, residual = chebyshev(residual, apply_fine, dinv, CHEB_FINE, True)
        solution = solution + update
        smoothed = residual - OMEGA * apply_fine(dinv * residual)
        coarse_rhs = jnp.einsum("ra,rn->an", onehot, smoothed, precision=highest)
        result, unused = chebyshev(coarse_rhs, apply_coarse, coarse_inverse, CHEB_COARSE, False)
        spread = jnp.dot(onehot, result, precision=highest)
        correction = spread - OMEGA * dinv * apply_fine(spread)
        solution = solution + correction
        residual = residual - apply_fine(correction)
        update, residual = chebyshev(residual, apply_fine, dinv, CHEB_FINE, True)
        solution = solution + update
    return (solution, residual)


def solution(mesh):
    placed = (
        P(("grp", "sub"), None),
        P(None, ("grp", "sub")),
        P(None, ("grp", "sub")),
        P(("grp", "sub")),
        P(("grp", "sub")),
        P(("grp", "sub")),
        P("grp", "sub", None),
    )
    return jax.shard_map(
        body,
        mesh=mesh,
        in_specs=placed,
        out_specs=(P(("grp", "sub"), None), P(("grp", "sub"), None)),
        check_vma=False,
    )
```

profile of v0, /device:TPU:29, one launch (start us, length us, event | category | flops | bytes accessed | tf_op | source)
XLA Modules:
  0.0 596.2 jit_solution(620123093191027239)
XLA Ops:
  9.6 7.1 %collective-permute-start = (f32[64,128]{1,0:T(8,128)}, f32[64,128]{1,0:T(8,128)S(1)}, u32[]{:S(2)}, u32[]{:S(2)}) collective-permute-start(f32[64,128]{1,0:T(8,128)} %fusion.65), channel_id=1, source_target_pairs={{0,1},{1,2},{2,3},{3,4},{4,5},{5,6},{6,7},{7,8},{8,9},{9,10},{10,1... | collective-permute-start | bytes 98312 | tf_op jit(solution)/shard_map/ppermute | solution.py:18
  21.6 47.7 %select_add_fusion = f32[16,128,256]{2,1,0:T(8,128)S(1)} fusion(f32[16,128]{1,0:T(8,128)S(1)} %bitcast.486, s32[16,128]{1,0:T(8,128)} %bitcast.608, f32[16,128]{1,0:T(8,128)S(1)} %bitcast.487, s32[16,128]{1,0:T(8,128)} %bitcast.609, f32[16,128]{1,0:T(8,128)S(1)} %bitcast.465, s32[16,128]{1,0:T(8,128)} %bitcast.610, f32[16,128]{1,0:T(8,128)S(1)} %bitcast.466, ...), kind=kLoop, calls=%fused_computation.1 | loop fusion | flops 126877696 | bytes 3424256 | tf_op jit(solution)/shard_map/add | solution.py:29
  82.1 5.4 collective-permute-done.3
  93.6 3.6 collective-permute-start.5
  97.2 5.2 collective-permute-done.5
  107.1 26.0 %all_gather.30 = f32[1024,128]{1,0:T(8,128)S(1)} all-gather(f32[128,128]{1,0:T(8,128)S(1)} %get-tuple-element.209), channel_id=1, replica_groups=mesh['grp'=4,'sub'=8] {'sub'}, dimensions={0}, use_global_device_ids=true | all-gather | bytes 589824 | tf_op jit(solution)/shard_map/all_gather | solution.py:83
  133.8 25.7 %all_gather.31 = f32[1024,128]{1,0:T(8,128)S(1)} all-gather(f32[128,128]{1,0:T(8,128)S(1)} %get-tuple-element.211), channel_id=1, replica_groups=mesh['grp'=4,'sub'=8] {'sub'}, dimensions={0}, use_global_device_ids=true | all-gather | bytes 589824 | tf_op jit(solution)/shard_map/all_gather | solution.py:83
  160.1 25.7 %all_gather.32 = f32[1024,128]{1,0:T(8,128)S(1)} all-gather(f32[128,128]{1,0:T(8,128)S(1)} %get-tuple-element.213), channel_id=1, replica_groups=mesh['grp'=4,'sub'=8] {'sub'}, dimensions={0}, use_global_device_ids=true | all-gather | bytes 589824 | tf_op jit(solution)/shard_map/all_gather | solution.py:83
  186.5 25.4 %all_gather.33 = f32[1024,128]{1,0:T(8,128)S(1)} all-gather(f32[128,128]{1,0:T(8,128)S(1)} %get-tuple-element.215), channel_id=1, replica_groups=mesh['grp'=4,'sub'=8] {'sub'}, dimensions={0}, use_global_device_ids=true | all-gather | bytes 589824 | tf_op jit(solution)/shard_map/all_gather | solution.py:83
  212.5 25.6 %all_gather.34 = f32[1024,128]{1,0:T(8,128)S(1)} all-gather(f32[128,128]{1,0:T(8,128)S(1)} %get-tuple-element.217), channel_id=1, replica_groups=mesh['grp'=4,'sub'=8] {'sub'}, dimensions={0}, use_global_device_ids=true | all-gather | bytes 589824 | tf_op jit(solution)/shard_map/all_gather | solution.py:83
  240.8 30.2 %collective-permute-start.6 = (f32[64,128]{1,0:T(8,128)S(1)}, f32[64,128]{1,0:T(8,128)S(1)}, u32[]{:S(2)}, u32[]{:S(2)}) collective-permute-start(f32[64,128]{1,0:T(8,128)S(1)} %fusion.62), channel_id=1, source_target_pairs={{0,1},{1,2},{2,3},{3,4},{4,5},{5,6},{6,7},{7,8},{8,9},{9,10},{10,1... | collective-permute-start | bytes 98312 | tf_op jit(solution)/shard_map/ppermute | solution.py:18
  273.2 6.6 %collective-permute-done.7 = f32[64,128]{1,0:T(8,128)S(1)} collective-permute-done((f32[64,128]{1,0:T(8,128)S(1)}, f32[64,128]{1,0:T(8,128)S(1)}, u32[]{:S(2)}, u32[]{:S(2)}) %collective-permute-start.7) | collective-permute-done | bytes 32800 | tf_op jit(solution)/shard_map/ppermute | solution.py:18
  289.3 5.4 collective-permute-done.9
  300.7 3.8 collective-permute-start.11
  304.5 5.0 collective-permute-done.11
  318.9 5.4 collective-permute-done.13
  330.3 3.5 collective-permute-start.15
  333.9 5.3 collective-permute-done.15
  348.6 5.4 collective-permute-done.17
  360.0 3.6 collective-permute-start.19
  363.6 5.2 collective-permute-done.19
  373.0 24.9 %all_gather.35 = f32[1024,128]{1,0:T(8,128)S(1)} all-gather(f32[128,128]{1,0:T(8,128)S(1)} %get-tuple-element.219), channel_id=1, replica_groups=mesh['grp'=4,'sub'=8] {'sub'}, dimensions={0}, use_global_device_ids=true | all-gather | bytes 589824 | tf_op jit(solution)/shard_map/all_gather | solution.py:83
  398.5 25.4 %all_gather.36 = f32[1024,128]{1,0:T(8,128)S(1)} all-gather(f32[128,128]{1,0:T(8,128)S(1)} %get-tuple-element.221), channel_id=1, replica_groups=mesh['grp'=4,'sub'=8] {'sub'}, dimensions={0}, use_global_device_ids=true | all-gather | bytes 589824 | tf_op jit(solution)/shard_map/all_gather | solution.py:83
  424.6 26.1 %all_gather.37 = f32[1024,128]{1,0:T(8,128)S(1)} all-gather(f32[128,128]{1,0:T(8,128)S(1)} %get-tuple-element.223), channel_id=1, replica_groups=mesh['grp'=4,'sub'=8] {'sub'}, dimensions={0}, use_global_device_ids=true | all-gather | bytes 589824 | tf_op jit(solution)/shard_map/all_gather | solution.py:83
  451.3 25.9 %all_gather.38 = f32[1024,128]{1,0:T(8,128)S(1)} all-gather(f32[128,128]{1,0:T(8,128)S(1)} %get-tuple-element.225), channel_id=1, replica_groups=mesh['grp'=4,'sub'=8] {'sub'}, dimensions={0}, use_global_device_ids=true | all-gather | bytes 589824 | tf_op jit(solution)/shard_map/all_gather | solution.py:83
  477.8 25.3 %all_gather.39 = f32[1024,128]{1,0:T(8,128)S(1)} all-gather(f32[128,128]{1,0:T(8,128)S(1)} %get-tuple-element.227), channel_id=1, replica_groups=mesh['grp'=4,'sub'=8] {'sub'}, dimensions={0}, use_global_device_ids=true | all-gather | bytes 589824 | tf_op jit(solution)/shard_map/all_gather | solution.py:83
  505.8 31.2 %collective-permute-start.20 = (f32[64,128]{1,0:T(8,128)S(1)}, f32[64,128]{1,0:T(8,128)S(1)}, u32[]{:S(2)}, u32[]{:S(2)}) collective-permute-start(f32[64,128]{1,0:T(8,128)S(1)} %fusion.55), channel_id=1, source_target_pairs={{0,1},{1,2},{2,3},{3,4},{4,5},{5,6},{6,7},{7,8},{8,9},{9,10},{10,1... | collective-permute-start | bytes 98312 | tf_op jit(solution)/shard_map/ppermute | solution.py:18
  539.3 6.6 %collective-permute-done.21 = f32[64,128]{1,0:T(8,128)S(1)} collective-permute-done((f32[64,128]{1,0:T(8,128)S(1)}, f32[64,128]{1,0:T(8,128)S(1)}, u32[]{:S(2)}, u32[]{:S(2)}) %collective-permute-start.21) | collective-permute-done | bytes 32800 | tf_op jit(solution)/shard_map/ppermute | solution.py:18
  555.3 5.6 collective-permute-done.23
  566.9 3.7 collective-permute-start.25
  570.5 5.2 collective-permute-done.25
  586.5 5.4 collective-permute-done.27
  (168 shorter events, 131.6 us)
Async XLA Ops:
  0.6 21.0 %copy-start = (f32[1,128,1024]{2,1,0:T(8,128)S(1)}, f32[1,128,1024]{2,1,0:T(8,128)}, u32[]{:S(2)}) copy-start(f32[1,128,1024]{2,1,0:T(8,128)} %param.13) | copy-start | bytes 1572868
  0.6 16.1 %copy-start.4 = (f32[81,2048]{1,0:T(8,128)S(1)}, f32[81,2048]{1,0:T(8,128)}, u32[]{:S(2)}) copy-start(f32[81,2048]{1,0:T(8,128)} %param.8) | copy-start | bytes 1990660
  0.7 16.5 %copy-start.3 = (s32[81,2048]{1,0:T(8,128)S(1)}, s32[81,2048]{1,0:T(8,128)}, u32[]{:S(2)}) copy-start(s32[81,2048]{1,0:T(8,128)} %param.9) | copy-start | bytes 1990660
  4.9 65.7 %collective-permute-start.1 = (f32[64,128]{1,0:T(8,128)}, f32[64,128]{1,0:T(8,128)S(1)}, u32[]{:S(2)}, u32[]{:S(2)}) collective-permute-start(f32[64,128]{1,0:T(8,128)} %fusion.51), channel_id=1, source_target_pairs={{1,0},{2,1},{3,2},{4,3},{5,4},{6,5},{7,6},{8,7},{9,8},{10,9},{11,1... | collective-permute-start | bytes 98312 | tf_op jit(solution)/shard_map/ppermute | solution.py:18
  9.6 10.7 %copy-start.1 = (f32[2048,128]{1,0:T(8,128)S(1)}, f32[2048,128]{1,0:T(8,128)}, u32[]{:S(2)}) copy-start(f32[2048,128]{1,0:T(8,128)} %param.7) | copy-start | bytes 3145732
  9.6 61.1 %collective-permute-start = (f32[64,128]{1,0:T(8,128)}, f32[64,128]{1,0:T(8,128)S(1)}, u32[]{:S(2)}, u32[]{:S(2)}) collective-permute-start(f32[64,128]{1,0:T(8,128)} %fusion.65), channel_id=1, source_target_pairs={{0,1},{1,2},{2,3},{3,4},{4,5},{5,6},{6,7},{7,8},{8,9},{9,10},{10,1... | collective-permute-start | bytes 98312 | tf_op jit(solution)/shard_map/ppermute | solution.py:18
  76.7 5.3 collective-permute-start.2
  78.7 8.8 %collective-permute-start.3 = (f32[64,128]{1,0:T(8,128)S(1)}, f32[64,128]{1,0:T(8,128)S(1)}, u32[]{:S(2)}, u32[]{:S(2)}) collective-permute-start(f32[64,128]{1,0:T(8,128)S(1)} %fusion.50), channel_id=1, source_target_pairs={{1,0},{2,1},{3,2},{4,3},{5,4},{6,5},{7,6},{8,7},{9,8},{10,9},{11,1... | collective-permute-start | bytes 98312 | tf_op jit(solution)/shard_map/ppermute | solution.py:18
  91.7 5.5 collective-permute-start.4
  93.6 8.8 %collective-permute-start.5 = (f32[64,128]{1,0:T(8,128)S(1)}, f32[64,128]{1,0:T(8,128)S(1)}, u32[]{:S(2)}, u32[]{:S(2)}) collective-permute-start(f32[64,128]{1,0:T(8,128)S(1)} %fusion.49), channel_id=1, source_target_pairs={{1,0},{2,1},{3,2},{4,3},{5,4},{6,5},{7,6},{8,7},{9,8},{10,9},{11,1... | collective-permute-start | bytes 98312 | tf_op jit(solution)/shard_map/ppermute | solution.py:18
  240.8 32.4 %collective-permute-start.6 = (f32[64,128]{1,0:T(8,128)S(1)}, f32[64,128]{1,0:T(8,128)S(1)}, u32[]{:S(2)}, u32[]{:S(2)}) collective-permute-start(f32[64,128]{1,0:T(8,128)S(1)} %fusion.62), channel_id=1, source_target_pairs={{0,1},{1,2},{2,3},{3,4},{4,5},{5,6},{6,7},{7,8},{8,9},{9,10},{10,1... | collective-permute-start | bytes 98312 | tf_op jit(solution)/shard_map/ppermute | solution.py:18
  271.0 8.8 %collective-permute-start.7 = (f32[64,128]{1,0:T(8,128)S(1)}, f32[64,128]{1,0:T(8,128)S(1)}, u32[]{:S(2)}, u32[]{:S(2)}) collective-permute-start(f32[64,128]{1,0:T(8,128)S(1)} %fusion.48), channel_id=1, source_target_pairs={{1,0},{2,1},{3,2},{4,3},{5,4},{6,5},{7,6},{8,7},{9,8},{10,9},{11,1... | collective-permute-start | bytes 98312 | tf_op jit(solution)/shard_map/ppermute | solution.py:18
  284.0 5.3 collective-permute-start.8
  285.9 8.8 %collective-permute-start.9 = (f32[64,128]{1,0:T(8,128)S(1)}, f32[64,128]{1,0:T(8,128)S(1)}, u32[]{:S(2)}, u32[]{:S(2)}) collective-permute-start(f32[64,128]{1,0:T(8,128)S(1)} %fusion.47), channel_id=1, source_target_pairs={{1,0},{2,1},{3,2},{4,3},{5,4},{6,5},{7,6},{8,7},{9,8},{10,9},{11,1... | collective-permute-start | bytes 98312 | tf_op jit(solution)/shard_map/ppermute | solution.py:18
  298.8 5.8 collective-permute-start.10
  300.7 8.8 %collective-permute-start.11 = (f32[64,128]{1,0:T(8,128)S(1)}, f32[64,128]{1,0:T(8,128)S(1)}, u32[]{:S(2)}, u32[]{:S(2)}) collective-permute-start(f32[64,128]{1,0:T(8,128)S(1)} %fusion.46), channel_id=1, source_target_pairs={{1,0},{2,1},{3,2},{4,3},{5,4},{6,5},{7,6},{8,7},{9,8},{10,9},{11,1... | collective-permute-start | bytes 98312 | tf_op jit(solution)/shard_map/ppermute | solution.py:18
  313.6 5.3 collective-permute-start.12
  315.5 8.8 %collective-permute-start.13 = (f32[64,128]{1,0:T(8,128)S(1)}, f32[64,128]{1,0:T(8,128)S(1)}, u32[]{:S(2)}, u32[]{:S(2)}) collective-permute-start(f32[64,128]{1,0:T(8,128)S(1)} %fusion.45), channel_id=1, source_target_pairs={{1,0},{2,1},{3,2},{4,3},{5,4},{6,5},{7,6},{8,7},{9,8},{10,9},{11,1... | collective-permute-start | bytes 98312 | tf_op jit(solution)/shard_map/ppermute | solution.py:18
  328.4 5.5 collective-permute-start.14
  330.3 8.8 %collective-permute-start.15 = (f32[64,128]{1,0:T(8,128)S(1)}, f32[64,128]{1,0:T(8,128)S(1)}, u32[]{:S(2)}, u32[]{:S(2)}) collective-permute-start(f32[64,128]{1,0:T(8,128)S(1)} %fusion.44), channel_id=1, source_target_pairs={{1,0},{2,1},{3,2},{4,3},{5,4},{6,5},{7,6},{8,7},{9,8},{10,9},{11,1... | collective-permute-start | bytes 98312 | tf_op jit(solution)/shard_map/ppermute | solution.py:18
  343.2 5.3 collective-permute-start.16
  345.2 8.8 %collective-permute-start.17 = (f32[64,128]{1,0:T(8,128)S(1)}, f32[64,128]{1,0:T(8,128)S(1)}, u32[]{:S(2)}, u32[]{:S(2)}) collective-permute-start(f32[64,128]{1,0:T(8,128)S(1)} %fusion.43), channel_id=1, source_target_pairs={{1,0},{2,1},{3,2},{4,3},{5,4},{6,5},{7,6},{8,7},{9,8},{10,9},{11,1... | collective-permute-start | bytes 98312 | tf_op jit(solution)/shard_map/ppermute | solution.py:18
  358.1 5.5 collective-permute-start.18
  360.0 8.8 %collective-permute-start.19 = (f32[64,128]{1,0:T(8,128)S(1)}, f32[64,128]{1,0:T(8,128)S(1)}, u32[]{:S(2)}, u32[]{:S(2)}) collective-permute-start(f32[64,128]{1,0:T(8,128)S(1)} %fusion.42), channel_id=1, source_target_pairs={{1,0},{2,1},{3,2},{4,3},{5,4},{6,5},{7,6},{8,7},{9,8},{10,9},{11,1... | collective-permute-start | bytes 98312 | tf_op jit(solution)/shard_map/ppermute | solution.py:18
  505.8 33.4 %collective-permute-start.20 = (f32[64,128]{1,0:T(8,128)S(1)}, f32[64,128]{1,0:T(8,128)S(1)}, u32[]{:S(2)}, u32[]{:S(2)}) collective-permute-start(f32[64,128]{1,0:T(8,128)S(1)} %fusion.55), channel_id=1, source_target_pairs={{0,1},{1,2},{2,3},{3,4},{4,5},{5,6},{6,7},{7,8},{8,9},{9,10},{10,1... | collective-permute-start | bytes 98312 | tf_op jit(solution)/shard_map/ppermute | solution.py:18
  537.1 8.8 %collective-permute-start.21 = (f32[64,128]{1,0:T(8,128)S(1)}, f32[64,128]{1,0:T(8,128)S(1)}, u32[]{:S(2)}, u32[]{:S(2)}) collective-permute-start(f32[64,128]{1,0:T(8,128)S(1)} %fusion.41), channel_id=1, source_target_pairs={{1,0},{2,1},{3,2},{4,3},{5,4},{6,5},{7,6},{8,7},{9,8},{10,9},{11,1... | collective-permute-start | bytes 98312 | tf_op jit(solution)/shard_map/ppermute | solution.py:18
  550.0 5.3 collective-permute-start.22
  551.9 8.9 %collective-permute-start.23 = (f32[64,128]{1,0:T(8,128)S(1)}, f32[64,128]{1,0:T(8,128)S(1)}, u32[]{:S(2)}, u32[]{:S(2)}) collective-permute-start(f32[64,128]{1,0:T(8,128)S(1)} %fusion.40), channel_id=1, source_target_pairs={{1,0},{2,1},{3,2},{4,3},{5,4},{6,5},{7,6},{8,7},{9,8},{10,9},{11,1... | collective-permute-start | bytes 98312 | tf_op jit(solution)/shard_map/ppermute | solution.py:18
  564.9 5.6 collective-permute-start.24
  566.9 8.8 %collective-permute-start.25 = (f32[64,128]{1,0:T(8,128)S(1)}, f32[64,128]{1,0:T(8,128)S(1)}, u32[]{:S(2)}, u32[]{:S(2)}) collective-permute-start(f32[64,128]{1,0:T(8,128)S(1)} %fusion.39), channel_id=1, source_target_pairs={{1,0},{2,1},{3,2},{4,3},{5,4},{6,5},{7,6},{8,7},{9,8},{10,9},{11,1... | collective-permute-start | bytes 98312 | tf_op jit(solution)/shard_map/ppermute | solution.py:18
  581.2 5.3 collective-permute-start.26
  583.1 8.8 %collective-permute-start.27 = (f32[64,128]{1,0:T(8,128)S(1)}, f32[64,128]{1,0:T(8,128)S(1)}, u32[]{:S(2)}, u32[]{:S(2)}) collective-permute-start(f32[64,128]{1,0:T(8,128)S(1)} %fusion.38), channel_id=1, source_target_pairs={{1,0},{2,1},{3,2},{4,3},{5,4},{6,5},{7,6},{8,7},{9,8},{10,9},{11,1... | collective-permute-start | bytes 98312 | tf_op jit(solution)/shard_map/ppermute | solution.py:18
  (4 other events, 4.2 us)
where the time goes:
time: 600 us; the launch traced here: 596 us
  blocking collectives  256 us (43%)
  starting transfers between devices  135 us (22%)
  waiting for transfers between devices  72 us (12%)
  matrix products  64.9 us (11%)
  other arithmetic  61.3 us (10%)
    all_gather x10, blocking collectives, apply_coarse(): whole = lax.all_gather(vector, 'sub', axis=0, tiled=True)  256 us
    ppermute x28, starting transfers between devices, from_behind(): return lax.ppermute(shard, axis, pairs)  135 us
    ppermute x28, waiting for transfers between devices, from_behind(): return lax.ppermute(shard, axis, pairs)  72 us
    add x1, other arithmetic, band_tiles(): tiles + jnp.where(local[entry][:, None] == places, fine_values[entry][:,...  47.7 us
    dot_general x14, matrix products, fine_apply(): jnp.einsum('brc,bcn->brn', low_tiles, pieces[:-1], precision=highest)  17.3 us
    dot_general x14, matrix products, fine_apply(): jnp.einsum('brc,bcn->brn', high_tiles, pieces[1:], precision=highest)  16.8 us
  transfers between devices with their start and end apart: 28, of which 13 were waited for; matrix products, arithmetic and copies ran while one was open for 9% of the time, Pallas kernels for 0%

commit v1 on v0

--- a/solution.py
+++ b/solution.py
@@ -80,7 +80,14 @@
     coarse_inverse = 1.0 / jnp.diagonal(block)[:, None]
 
     def apply_coarse(vector):
-        whole = lax.all_gather(vector, "sub", axis=0, tiled=True)
+        ring = [vector]
+        for hop in range(7):
+            ring.append(lax.ppermute(ring[-1], "sub", [(dev, (dev + 1) % 8) for dev in range(8)]))
+        whole = jnp.roll(
+            jnp.concatenate(ring[::-1], axis=0),
+            (lax.axis_index("sub") + 1) * ring[0].shape[0],
+            axis=0,
+        )
         return jnp.dot(own_rows, whole, precision=highest)
 
     dinv = 1.0 / fine_values[0][:, None]

time: 600 us -> 782 us (1.30)
  starting transfers between devices: 135 us -> 469 us
  blocking collectives: 256 us -> 0 us
  waiting for transfers between devices: 72 us -> 171 us
    ppermute x0 -> x70, starting transfers between devices: none -> 305 us  [apply_coarse(): lax.ppermute(ring[-1], 'sub', [(dev, (dev + 1) % 8) for dev in range(8)])]
    all_gather x10 -> x0, blocking collectives: 256 us -> none  [apply_coarse(): whole = lax.all_gather(vector, 'sub', axis=0, tiled=True)]
    ppermute x0 -> x70, waiting for transfers between devices: none -> 99.8 us  [apply_coarse(): lax.ppermute(ring[-1], 'sub', [(dev, (dev + 1) % 8) for dev in range(8)])]
    ppermute x28, starting transfers between devices: 135 us -> 164 us  [from_behind(): return lax.ppermute(shard, axis, pairs)]
  transfers between devices with their start and end apart: 28 -> 98, of which waited for: 13 -> 83; matrix products, arithmetic and copies ran while one was open for 9% -> 7% of each run, Pallas kernels for 0% -> 0%
where the time goes in v1:
time: 782 us; the launch traced here: 778 us
  starting transfers between devices  469 us (60%)
  waiting for transfers between devices  171 us (22%)
  matrix products  67 us (9%)
  other arithmetic  61.8 us (8%)
    ppermute x70, starting transfers between devices, apply_coarse(): lax.ppermute(ring[-1], 'sub', [(dev, (dev + 1) % 8) for dev in range(8)])  305 us
    ppermute x28, starting transfers between devices, from_behind(): return lax.ppermute(shard, axis, pairs)  164 us
    ppermute x70, waiting for transfers between devices, apply_coarse(): lax.ppermute(ring[-1], 'sub', [(dev, (dev + 1) % 8) for dev in range(8)])  99.8 us
    ppermute x28, waiting for transfers between devices, from_behind(): return lax.ppermute(shard, axis, pairs)  71.1 us
    add x1, other arithmetic, band_tiles(): tiles + jnp.where(local[entry][:, None] == places, fine_values[entry][:,...  46.7 us
    dot_general x14, matrix products, fine_apply(): jnp.einsum('brc,bcn->brn', low_tiles, pieces[:-1], precision=highest)  17.3 us
    dot_general x14, matrix products, fine_apply(): jnp.einsum('brc,bcn->brn', high_tiles, pieces[1:], precision=highest)  16.7 us
  transfers between devices with their start and end apart: 98, of which 83 were waited for; matrix products, arithmetic and copies ran while one was open for 7% of the time, Pallas kernels for 0%

profile of v1, /device:TPU:29, one launch (start us, length us, event | category | flops | bytes accessed | tf_op | source)
XLA Modules:
  0.0 778.3 jit_solution(14343688523462818853)
XLA Ops:
  9.5 7.1 collective-permute-start
  21.5 46.7 %select_add_fusion = f32[16,128,256]{2,1,0:T(8,128)S(1)} fusion(f32[16,128]{1,0:T(8,128)S(1)} %bitcast.476, s32[16,128]{1,0:T(8,128)} %bitcast.598, f32[16,128]{1,0:T(8,128)S(1)} %bitcast.477, s32[16,128]{1,0:T(8,128)} %bitcast.599, f32[16,128]{1,0:T(8,128)S(1)} %bitcast.455, s32[16,128]{1,0:T(8,128)} %bitcast.600, f32[16,128]{1,0:T(8,128)S(1)} %bitcast.456, ...), kind=kLoop, calls=%fused_computation.1 | loop fusion | flops 126877696 | bytes 3424256 | tf_op jit(solution)/shard_map/add | solution.py:29
  97.2 5.0 collective-permute-done.5
  119.9 5.0 collective-permute-start.9
  144.7 4.5 collective-permute-start.13
  156.9 4.9 collective-permute-start.15
  187.4 4.5 collective-permute-start.20
  199.5 4.7 collective-permute-start.22
  229.9 4.7 collective-permute-start.27
  236.2 4.6 collective-permute-start.28
  265.5 4.6 collective-permute-start.33
  307.3 5.0 collective-permute-start.40
  316.7 45.2 %collective-permute-start.41 = (f32[64,128]{1,0:T(8,128)S(1)}, f32[64,128]{1,0:T(8,128)S(1)}, u32[]{:S(2)}, u32[]{:S(2)}) collective-permute-start(f32[64,128]{1,0:T(8,128)S(1)} %fusion.82), channel_id=1, source_target_pairs={{0,1},{1,2},{2,3},{3,4},{4,5},{5,6},{6,7},{7,8},{8,9},{9,10},{10,1... | collective-permute-start | bytes 98312 | tf_op jit(solution)/shard_map/ppermute | solution.py:18
  363.9 6.9 collective-permute-done.42
  380.1 5.4 collective-permute-done.44
  395.1 5.3 collective-permute-done.46
  409.9 5.4 collective-permute-done.48
  425.1 5.0 collective-permute-done.50
  439.5 5.4 collective-permute-done.52
  454.5 5.3 collective-permute-done.54
  494.9 4.9 collective-permute-start.61
  531.5 4.6 collective-permute-start.67
  567.7 4.6 collective-permute-start.73
  586.3 4.5 collective-permute-start.76
  604.0 4.6 collective-permute-start.79
  646.2 4.7 collective-permute-start.86
  663.8 4.7 collective-permute-start.89
  672.9 46.3 %collective-permute-start.90 = (f32[64,128]{1,0:T(8,128)S(1)}, f32[64,128]{1,0:T(8,128)S(1)}, u32[]{:S(2)}, u32[]{:S(2)}) collective-permute-start(f32[64,128]{1,0:T(8,128)S(1)} %fusion.75), channel_id=1, source_target_pairs={{0,1},{1,2},{2,3},{3,4},{4,5},{5,6},{6,7},{7,8},{8,9},{9,10},{10,1... | collective-permute-start | bytes 98312 | tf_op jit(solution)/shard_map/ppermute | solution.py:18
  721.2 6.9 collective-permute-done.91
  737.4 5.4 collective-permute-done.93
  752.5 5.2 collective-permute-done.95
  768.8 5.4 collective-permute-done.97
  (394 shorter events, 488.2 us)
Async XLA Ops:
  4.9 63.4 %collective-permute-start.1 = (f32[64,128]{1,0:T(8,128)}, f32[64,128]{1,0:T(8,128)S(1)}, u32[]{:S(2)}, u32[]{:S(2)}) collective-permute-start(f32[64,128]{1,0:T(8,128)} %fusion.71), channel_id=1, source_target_pairs={{1,0},{2,1},{3,2},{4,3},{5,4},{6,5},{7,6},{8,7},{9,8},{10,9},{11,1... | collective-permute-start | bytes 98312 | tf_op jit(solution)/shard_map/ppermute | solution.py:18
  9.5 58.8 %collective-permute-start = (f32[64,128]{1,0:T(8,128)}, f32[64,128]{1,0:T(8,128)S(1)}, u32[]{:S(2)}, u32[]{:S(2)}) collective-permute-start(f32[64,128]{1,0:T(8,128)} %fusion.85), channel_id=1, source_target_pairs={{0,1},{1,2},{2,3},{3,4},{4,5},{5,6},{6,7},{7,8},{8,9},{9,10},{10,1... | collective-permute-start | bytes 98312 | tf_op jit(solution)/shard_map/ppermute | solution.py:18
  74.8 6.6 collective-permute-start.2
  76.8 8.8 %collective-permute-start.3 = (f32[64,128]{1,0:T(8,128)S(1)}, f32[64,128]{1,0:T(8,128)S(1)}, u32[]{:S(2)}, u32[]{:S(2)}) collective-permute-start(f32[64,128]{1,0:T(8,128)S(1)} %fusion.70), channel_id=1, source_target_pairs={{1,0},{2,1},{3,2},{4,3},{5,4},{6,5},{7,6},{8,7},{9,8},{10,9},{11,1... | collective-permute-start | bytes 98312 | tf_op jit(solution)/shard_map/ppermute | solution.py:18
  93.4 8.8 %collective-permute-start.5 = (f32[64,128]{1,0:T(8,128)S(1)}, f32[64,128]{1,0:T(8,128)S(1)}, u32[]{:S(2)}, u32[]{:S(2)}) collective-permute-start(f32[64,128]{1,0:T(8,128)S(1)} %fusion.69), channel_id=1, source_target_pairs={{1,0},{2,1},{3,2},{4,3},{5,4},{6,5},{7,6},{8,7},{9,8},{10,9},{11,1... | collective-permute-start | bytes 98312 | tf_op jit(solution)/shard_map/ppermute | solution.py:18
  119.9 6.4 collective-permute-start.9
  150.6 6.3 collective-permute-start.14
  156.9 6.2 collective-permute-start.15
  193.3 6.3 collective-permute-start.21
  199.5 6.0 collective-permute-start.22
  229.9 6.3 collective-permute-start.27
  307.3 6.3 collective-permute-start.40
  316.7 47.1 %collective-permute-start.41 = (f32[64,128]{1,0:T(8,128)S(1)}, f32[64,128]{1,0:T(8,128)S(1)}, u32[]{:S(2)}, u32[]{:S(2)}) collective-permute-start(f32[64,128]{1,0:T(8,128)S(1)} %fusion.82), channel_id=1, source_target_pairs={{0,1},{1,2},{2,3},{3,4},{4,5},{5,6},{6,7},{7,8},{8,9},{9,10},{10,1... | collective-permute-start | bytes 98312 | tf_op jit(solution)/shard_map/ppermute | solution.py:18
  361.9 8.8 %collective-permute-start.42 = (f32[64,128]{1,0:T(8,128)S(1)}, f32[64,128]{1,0:T(8,128)S(1)}, u32[]{:S(2)}, u32[]{:S(2)}) collective-permute-start(f32[64,128]{1,0:T(8,128)S(1)} %fusion.68), channel_id=1, source_target_pairs={{1,0},{2,1},{3,2},{4,3},{5,4},{6,5},{7,6},{8,7},{9,8},{10,9},{11,1... | collective-permute-start | bytes 98312 | tf_op jit(solution)/shard_map/ppermute | solution.py:18
  376.7 8.8 %collective-permute-start.44 = (f32[64,128]{1,0:T(8,128)S(1)}, f32[64,128]{1,0:T(8,128)S(1)}, u32[]{:S(2)}, u32[]{:S(2)}) collective-permute-start(f32[64,128]{1,0:T(8,128)S(1)} %fusion.67), channel_id=1, source_target_pairs={{1,0},{2,1},{3,2},{4,3},{5,4},{6,5},{7,6},{8,7},{9,8},{10,9},{11,1... | collective-permute-start | bytes 98312 | tf_op jit(solution)/shard_map/ppermute | solution.py:18
  391.5 8.9 %collective-permute-start.46 = (f32[64,128]{1,0:T(8,128)S(1)}, f32[64,128]{1,0:T(8,128)S(1)}, u32[]{:S(2)}, u32[]{:S(2)}) collective-permute-start(f32[64,128]{1,0:T(8,128)S(1)} %fusion.66), channel_id=1, source_target_pairs={{1,0},{2,1},{3,2},{4,3},{5,4},{6,5},{7,6},{8,7},{9,8},{10,9},{11,1... | collective-permute-start | bytes 98312 | tf_op jit(solution)/shard_map/ppermute | solution.py:18
  406.5 8.8 %collective-permute-start.48 = (f32[64,128]{1,0:T(8,128)S(1)}, f32[64,128]{1,0:T(8,128)S(1)}, u32[]{:S(2)}, u32[]{:S(2)}) collective-permute-start(f32[64,128]{1,0:T(8,128)S(1)} %fusion.65), channel_id=1, source_target_pairs={{1,0},{2,1},{3,2},{4,3},{5,4},{6,5},{7,6},{8,7},{9,8},{10,9},{11,1... | collective-permute-start | bytes 98312 | tf_op jit(solution)/shard_map/ppermute | solution.py:18
  421.3 8.8 %collective-permute-start.50 = (f32[64,128]{1,0:T(8,128)S(1)}, f32[64,128]{1,0:T(8,128)S(1)}, u32[]{:S(2)}, u32[]{:S(2)}) collective-permute-start(f32[64,128]{1,0:T(8,128)S(1)} %fusion.64), channel_id=1, source_target_pairs={{1,0},{2,1},{3,2},{4,3},{5,4},{6,5},{7,6},{8,7},{9,8},{10,9},{11,1... | collective-permute-start | bytes 98312 | tf_op jit(solution)/shard_map/ppermute | solution.py:18
  436.1 8.8 %collective-permute-start.52 = (f32[64,128]{1,0:T(8,128)S(1)}, f32[64,128]{1,0:T(8,128)S(1)}, u32[]{:S(2)}, u32[]{:S(2)}) collective-permute-start(f32[64,128]{1,0:T(8,128)S(1)} %fusion.63), channel_id=1, source_target_pairs={{1,0},{2,1},{3,2},{4,3},{5,4},{6,5},{7,6},{8,7},{9,8},{10,9},{11,1... | collective-permute-start | bytes 98312 | tf_op jit(solution)/shard_map/ppermute | solution.py:18
  451.0 8.8 %collective-permute-start.54 = (f32[64,128]{1,0:T(8,128)S(1)}, f32[64,128]{1,0:T(8,128)S(1)}, u32[]{:S(2)}, u32[]{:S(2)}) collective-permute-start(f32[64,128]{1,0:T(8,128)S(1)} %fusion.62), channel_id=1, source_target_pairs={{1,0},{2,1},{3,2},{4,3},{5,4},{6,5},{7,6},{8,7},{9,8},{10,9},{11,1... | collective-permute-start | bytes 98312 | tf_op jit(solution)/shard_map/ppermute | solution.py:18
  488.5 6.3 collective-permute-start.60
  494.9 6.2 collective-permute-start.61
  525.4 6.1 collective-permute-start.66
  561.7 6.0 collective-permute-start.72
  598.0 6.0 collective-permute-start.78
  640.1 6.1 collective-permute-start.85
  663.8 6.0 collective-permute-start.89
  672.9 48.2 %collective-permute-start.90 = (f32[64,128]{1,0:T(8,128)S(1)}, f32[64,128]{1,0:T(8,128)S(1)}, u32[]{:S(2)}, u32[]{:S(2)}) collective-permute-start(f32[64,128]{1,0:T(8,128)S(1)} %fusion.75), channel_id=1, source_target_pairs={{0,1},{1,2},{2,3},{3,4},{4,5},{5,6},{6,7},{7,8},{8,9},{9,10},{10,1... | collective-permute-start | bytes 98312 | tf_op jit(solution)/shard_map/ppermute | solution.py:18
  719.2 8.8 %collective-permute-start.91 = (f32[64,128]{1,0:T(8,128)S(1)}, f32[64,128]{1,0:T(8,128)S(1)}, u32[]{:S(2)}, u32[]{:S(2)}) collective-permute-start(f32[64,128]{1,0:T(8,128)S(1)} %fusion.61), channel_id=1, source_target_pairs={{1,0},{2,1},{3,2},{4,3},{5,4},{6,5},{7,6},{8,7},{9,8},{10,9},{11,1... | collective-permute-start | bytes 98312 | tf_op jit(solution)/shard_map/ppermute | solution.py:18
  734.0 8.8 %collective-permute-start.93 = (f32[64,128]{1,0:T(8,128)S(1)}, f32[64,128]{1,0:T(8,128)S(1)}, u32[]{:S(2)}, u32[]{:S(2)}) collective-permute-start(f32[64,128]{1,0:T(8,128)S(1)} %fusion.60), channel_id=1, source_target_pairs={{1,0},{2,1},{3,2},{4,3},{5,4},{6,5},{7,6},{8,7},{9,8},{10,9},{11,1... | collective-permute-start | bytes 98312 | tf_op jit(solution)/shard_map/ppermute | solution.py:18
  748.8 8.8 %collective-permute-start.95 = (f32[64,128]{1,0:T(8,128)S(1)}, f32[64,128]{1,0:T(8,128)S(1)}, u32[]{:S(2)}, u32[]{:S(2)}) collective-permute-start(f32[64,128]{1,0:T(8,128)S(1)} %fusion.59), channel_id=1, source_target_pairs={{1,0},{2,1},{3,2},{4,3},{5,4},{6,5},{7,6},{8,7},{9,8},{10,9},{11,1... | collective-permute-start | bytes 98312 | tf_op jit(solution)/shard_map/ppermute | solution.py:18
  765.4 8.8 %collective-permute-start.97 = (f32[64,128]{1,0:T(8,128)S(1)}, f32[64,128]{1,0:T(8,128)S(1)}, u32[]{:S(2)}, u32[]{:S(2)}) collective-permute-start(f32[64,128]{1,0:T(8,128)S(1)} %fusion.58), channel_id=1, source_target_pairs={{1,0},{2,1},{3,2},{4,3},{5,4},{6,5},{7,6},{8,7},{9,8},{10,9},{11,1... | collective-permute-start | bytes 98312 | tf_op jit(solution)/shard_map/ppermute | solution.py:18
  (82 other events, 511.8 us)
